TPU v7x, 32 devices: a whole 2x2x4 slice. The times are simulated.
32 devices in a mesh: groups: 2 (over y), seq: 16 (over z, x, core).
Axes of the slice: x: 2, y: 2, z: 4, core: 2. Of those that a mesh axis runs over, the one named last changes fastest.
Arguments:
- queries: bfloat16 [8192, 2048], P(('groups', 'seq')), parts along dimension 0, may hold values from -6 to 6
- key_inputs: bfloat16 [8192, 2048], P(('groups', 'seq')), parts along dimension 0, may hold values from -6 to 6
- values: bfloat16 [8192, 2048], P(('groups', 'seq')), parts along dimension 0, may hold values from -6 to 6
- short_taps: float32 [3, 3, 2048], replicated, may hold values from -3.6 to 3.6
- decay_rates: float32 [2, 2048], replicated, may hold values from 2.4414063e-05 to 0.05, as said below
- residues: float32 [2, 2048], replicated, may hold values from -6 to 6
- skip_gain: float32 [2048], replicated, may hold values from -6 to 6
- out_weight: bfloat16 [2048, 4096], P('seq'), may hold values from -0.125 to 0.125
- cotangent: bfloat16 [8192, 4096], P(('groups', 'seq')), parts along dimension 0, may hold values from -6 to 6
- doc_blocks: int32 [8], P('groups'), parts along dimension 0, may hold values from 1 to 16, 32 in all
Outputs:
- mixed_out: bfloat16 [8192, 4096], P(('groups', 'seq')), parts along dimension 0
- grad_queries: bfloat16 [8192, 2048], P(('groups', 'seq')), parts along dimension 0
- grad_keys: bfloat16 [8192, 2048], P(('groups', 'seq')), parts along dimension 0
- grad_values: bfloat16 [8192, 2048], P(('groups', 'seq')), parts along dimension 0
There are 2 independent parts, one for each index of `groups`. A program takes and returns all parts, laid end to end along the dimension named above; an argument that names none is the same for every part. Nothing has to cross between parts.
Inputs may be any that keep to these rules, and one draw needn't show every extreme that they name: `doc_blocks`: documents fill the batch in order: the entries sum to 32, and the longest is exactly 16 blocks. `decay_rates`: positive decay rates.
All inputs are finite; a program needn't handle non-finite values.
Results may differ from a plain program's by a relative error of at most 0.0051.
Values may be sent and summed in bfloat16 or wider, within the bound.
A program may use at most 128 MiB of HBM per device.

v0:
```python
import jax
import jax.numpy as jnp
from jax import lax
from jax.sharding import PartitionSpec as P

BLOCK = 128
exact_mode = lax.Precision.HIGHEST


def from_behind(value, axis, steps):
    count = lax.axis_size(axis)
    leading, last = (max(0, -steps), min(count, count - steps))
    return lax.ppermute(value, axis, [(source, source + steps) for source in range(leading, last)])


def combine(earlier, later):
    return (earlier[0] * later[0], later[0] * earlier[1] + later[1])


def block_marks(doc_blocks, first_block, block_count):
    doc_ends = jnp.cumsum(doc_blocks)
    starts = doc_ends - doc_blocks
    block_index = first_block + jnp.arange(block_count, dtype=jnp.int32)
    matches = (block_index[:, None] == starts[None, :]) | (block_index[:, None] >= doc_ends[-1])
    return jnp.any(matches, axis=1).astype(jnp.float32)


def block_parts(blocked, decay_rates, reset_flags):
    span = blocked.shape[-1]
    offsets = jnp.arange(span, dtype=jnp.float32)
    upper_ones = (offsets[:, None] <= offsets[None, :]).astype(jnp.float32)
    growth = jnp.exp(decay_rates[:, :, None] * offsets[None, None, :])
    shrink = jnp.exp(-decay_rates[:, :, None] * offsets[None, None, :])
    lifted = blocked[None, :, :, :] * growth[:, :, None, :]
    inside = (
        jnp.einsum("sgbp,pt->sgbt", lifted, upper_ones, precision=exact_mode)
        * shrink[:, :, None, :]
    )
    keep_rate = (1.0 - reset_flags)[None, None, :] * jnp.exp(-decay_rates * span)[:, :, None]
    cum_keep, cum_ends = lax.associative_scan(combine, (keep_rate, inside[..., -1]), axis=2)
    return (inside, cum_keep, cum_ends)


def block_finish(inside, cum_keep, cum_ends, decay_rates, filter_weight, reset_flags, incoming):
    span = inside.shape[-1]
    at_end = cum_keep * incoming[:, :, None] + cum_ends
    before = (
        jnp.concatenate([incoming[:, :, None], at_end[:, :, :-1]], axis=2)
        * (1.0 - reset_flags)[None, None, :]
    )
    offsets = jnp.arange(1, span + 1, dtype=jnp.float32)
    decay_rows = jnp.exp(-decay_rates[:, :, None] * offsets[None, None, :])
    summed_up = inside + before[..., None] * decay_rows[:, :, None, :]
    return jnp.sum(summed_up * filter_weight[:, :, None, None], axis=0)


def relay_pass(columns, decay_rates, filter_weight, doc_blocks, backward):
    device_place = lax.axis_index("seq")
    spread = lax.all_to_all(columns, "seq", split_axis=0, concat_axis=1, tiled=True)
    share_width = spread.shape[0]
    block_count = spread.shape[1] // BLOCK
    own_rates = lax.dynamic_slice_in_dim(decay_rates, device_place * share_width, share_width, 1)
    own_weights = lax.dynamic_slice_in_dim(
        filter_weight, device_place * share_width, share_width, 1
    )
    lead_shift = 1 if backward else 0
    reset_flags = block_marks(doc_blocks, lead_shift, block_count)
    blocked = spread.reshape(share_width, block_count, BLOCK)
    if backward:
        blocked = jnp.flip(blocked, axis=(1, 2))
        reset_flags = jnp.flip(reset_flags, axis=0)
    inside, cum_keep, cum_ends = block_parts(blocked, own_rates, reset_flags)
    zero_state = jnp.zeros(own_rates.shape, jnp.float32)
    result = block_finish(
        inside, cum_keep, cum_ends, own_rates, own_weights, reset_flags, zero_state
    )
    if backward:
        result = jnp.flip(result, axis=(1, 2))
    return lax.all_to_all(
        result.reshape(share_width, block_count * BLOCK),
        "seq",
        split_axis=1,
        concat_axis=0,
        tiled=True,
    )


def long_conv(columns, decay_rates, filter_weight, doc_blocks, backward):
    return relay_pass(columns, decay_rates, filter_weight, doc_blocks, backward)


def on_device(
    queries,
    key_inputs,
    values,
    short_taps,
    decay_rates,
    residues,
    skip_gain,
    out_weight,
    cotangent,
    doc_blocks,
):
    row_count = queries.shape[0]
    block_count = row_count // BLOCK
    marks_ext = block_marks(doc_blocks, lax.axis_index("seq") * block_count, block_count + 1)
    head_mask = (jnp.arange(BLOCK) == 0).astype(jnp.float32)
    begins = (marks_ext[:, None] * head_mask[None, :]).reshape(-1)[: row_count + 2]
    now_start = begins[:row_count]
    prior_start = jnp.concatenate([jnp.zeros((1,), jnp.float32), now_start[:-1]])
    keep_one = (1.0 - now_start)[:, None]
    keep_two = keep_one * (1.0 - prior_start)[:, None]
    next_one = (1.0 - begins[1 : row_count + 1])[:, None]
    next_two = next_one * (1.0 - begins[2 : row_count + 2])[:, None]
    tail_rows = jnp.stack(
        [queries[row_count - 2 :], key_inputs[row_count - 2 :], values[row_count - 2 :]]
    )
    prev_rims = from_behind(tail_rows, "seq", 1)

    def forward_short(current, rim_rows, tap_row):
        longer = jnp.concatenate([rim_rows, current], axis=0).astype(jnp.float32)
        return (
            tap_row[0] * longer[2:]
            + tap_row[1] * keep_one * longer[1:-1]
            + tap_row[2] * keep_two * longer[:-2]
        )

    q_short = forward_short(queries, prev_rims[0], short_taps[0])
    k_short = forward_short(key_inputs, prev_rims[1], short_taps[1])
    v_short = forward_short(values, prev_rims[2], short_taps[2])
    product = k_short * v_short
    filter_weight = residues * jnp.sqrt(2.0 * decay_rates)
    conv_out = (
        long_conv(product.T, decay_rates, filter_weight, doc_blocks, False).T + skip_gain * product
    )
    gated_rows = (q_short * conv_out).astype(jnp.bfloat16)
    weight_piece = lax.all_gather(out_weight, "seq", axis=0, tiled=True)
    total_out = jnp.dot(gated_rows, weight_piece, preferred_element_type=jnp.float32)
    column = lax.dot_general(
        cotangent, weight_piece, (((1,), (1,)), ((), ())), preferred_element_type=jnp.float32
    )
    total_out, grad_gated = (total_out, column)
    mixed_out = total_out.astype(jnp.bfloat16)
    grad_qs = grad_gated * conv_out
    grad_conv = grad_gated * q_short
    grad_product = (
        long_conv(grad_conv.T, decay_rates, filter_weight, doc_blocks, True).T
        + skip_gain * grad_conv
    )
    grad_ks = grad_product * v_short
    grad_vs = grad_product * k_short
    head_rows = jnp.stack([grad_qs[:2], grad_ks[:2], grad_vs[:2]])
    next_rims = from_behind(head_rows.astype(jnp.bfloat16), "seq", -1).astype(head_rows.dtype)

    def backward_short(gradient, rim_rows, tap_row):
        longer = jnp.concatenate([gradient, rim_rows], axis=0)
        summed = (
            tap_row[0] * gradient
            + tap_row[1] * next_one * longer[1 : row_count + 1]
            + tap_row[2] * next_two * longer[2:]
        )
        return summed.astype(jnp.bfloat16)

    grad_queries = backward_short(grad_qs, next_rims[0], short_taps[0])
    grad_keys = backward_short(grad_ks, next_rims[1], short_taps[1])
    grad_values = backward_short(grad_vs, next_rims[2], short_taps[2])
    return (mixed_out, grad_queries, grad_keys, grad_values)


def solution(mesh):
    return jax.shard_map(
        on_device,
        mesh=mesh,
        in_specs=(
            P(("groups", "seq"), None),
            P(("groups", "seq"), None),
            P(("groups", "seq"), None),
            P(),
            P(),
            P(),
            P(),
            P("seq", None),
            P(("groups", "seq"), None),
            P("groups"),
        ),
        out_specs=(
            P(("groups", "seq"), None),
            P(("groups", "seq"), None),
            P(("groups", "seq"), None),
            P(("groups", "seq"), None),
        ),
        check_vma=False,
    )
```

profile of v0, /device:TPU:16, one launch (start us, length us, event | category | flops | bytes accessed | tf_op | source)
XLA Modules:
  0.0 414.4 jit_solution(16186817507365080882)
XLA Ops:
  9.6 1.9 collective-permute-start
  15.2 1.6 fusion.71
  18.2 3.1 multiply_bitcast_fusion.1
  21.4 1.5 copy.42
  22.9 6.6 %all-to-all-start = ((f32[16,128,256]{1,2,0:T(8,128)}), f32[16,128,256]{1,2,0:T(8,128)}, u32[]{:S(2)}, u32[]{:S(2)}) async-start(f32[16,128,256]{1,2,0:T(8,128)} %bitcast.121), calls=%async_computation | async-start | bytes 4194304 | tf_op jit(solution)/shard_map/all_to_all | solution.py:59
  30.3 1.3 dynamic-slice_multiply_fusion
  38.0 2.5 maximum_convert_fusion
  40.5 68.7 %all-to-all-done = f32[16,128,256]{1,2,0:T(8,128)} async-done(((f32[16,128,256]{1,2,0:T(8,128)}), f32[16,128,256]{1,2,0:T(8,128)}, u32[]{:S(2)}, u32[]{:S(2)}) %all-to-all-start) | async-done | bytes 2097184 | tf_op jit(solution)/shard_map/all_to_all | solution.py:59
  109.2 2.9 copy.23
  112.2 60.0 %all-gather.2.cloned.1.call-done = bf16[2048,4096]{1,0:T(8,128)(2,1)} async-done(((bf16[128,4096]{1,0:T(8,128)(2,1)}), bf16[2048,4096]{1,0:T(8,128)(2,1)}) %all-gather.2.cloned.1.call-update) | async-done | bytes 16777232 | tf_op jit(solution)/shard_map/all_gather | solution.py:137
  172.2 9.5 %fusion.82 = f32[256,2048]{1,0:T(8,128)} fusion(bf16[256,4096]{1,0:T(8,128)(2,1)S(1)} %copy-done, bf16[2048,4096]{1,0:T(8,128)(2,1)} %all-gather.2.cloned.1.call-done), kind=kOutput, calls=%fused_computation.202 | convolution fusion | flops 4294967296 | bytes 20971520 | tf_op jit(solution)/shard_map/dot_general | solution.py:139
  181.7 6.8 %multiply_bitcast_fusion = (f32[32,16,8,128]{3,2,1,0:T(8,128)S(1)}, f32[256,2048]{1,0:T(8,128)}) fusion(f32[256,2048]{1,0:T(8,128)} %fusion.82, f32[258,2048]{1,0:T(8,128)} %maximum_convert_fusion, f32[256]{0:T(256)S(1)} %copy-done.30, f32[2048]{0:T(1024)S(1)} %bitcast.143, f32[256]{0:T(256)S(1)} %copy-done.28, f32[2048]{0:T(1024)S(1)} %bitcast.145, ...), kind=kLoop, calls=%fused_computation.65 | loop fusion | flops 4194304 | bytes 12609536
  188.4 1.5 copy.41
  190.0 6.7 %all-to-all-start.2 = ((f32[16,128,256]{1,2,0:T(8,128)}), f32[16,128,256]{1,2,0:T(8,128)}, u32[]{:S(2)}, u32[]{:S(2)}) async-start(f32[16,128,256]{1,2,0:T(8,128)} %bitcast.120), calls=%async_computation.2 | async-start | bytes 4194304 | tf_op jit(solution)/shard_map/all_to_all | solution.py:59
  196.7 2.8 fusion.4
  199.6 2.0 copy-done.4
  202.9 41.5 %all-to-all-done.2 = f32[16,128,256]{1,2,0:T(8,128)} async-done(((f32[16,128,256]{1,2,0:T(8,128)}), f32[16,128,256]{1,2,0:T(8,128)}, u32[]{:S(2)}, u32[]{:S(2)}) %all-to-all-start.2) | async-done | bytes 2097184 | tf_op jit(solution)/shard_map/all_to_all | solution.py:59
  244.4 16.5 %rev.11 = f32[128,32,128]{0,2,1:T(8,128)} reverse(f32[128,32,128]{0,2,1:T(8,128)} %bitcast.32), dimensions={1,2} | reverse | bytes 4194304 | tf_op jit(solution)/shard_map/jit(_flip)/rev | solution.py:70
  260.9 1.9 copy.27
  262.9 2.8 fusion.7
  265.8 2.0 copy-done.5
  269.1 6.8 %multiply_reduce_fusion = (f32[128,32,128]{0,2,1:T(8,128)S(1)}, f32[128,32,128]{0,2,1:T(8,128)}) fusion(f32[2,128,32,128]{1,3,2,0:T(8,128)} %copy-done.5, f32[2,128,32]{1,2,0:T(8,128)S(1)} %pad_multiply_fusion, f32[2,128]{1,0:T(2,128)S(1)} %copy-done.33, f32[2,128,128]{1,2,0:T(8,128)S(1)} %get-tuple-element.90, f32[2,128,32,128]{1,3,2,0:T(8,128)} %copy-done.4, ...), kind=kLoop, calls=%fused_computation.1 | loop fusion | flops 7340032 | bytes 12780544 | tf_op jit(solution)/shard_map/reduce_sum | solution.py:54
  275.9 4.7 %all-to-all-start.1 = ((f32[128,16,256]{0,2,1:T(8,128)}), f32[128,16,256]{0,2,1:T(8,128)}, u32[]{:S(2)}, u32[]{:S(2)}) async-start(f32[128,16,256]{0,2,1:T(8,128)} %bitcast.119), calls=%async_computation.1 | async-start | bytes 4194304 | tf_op jit(solution)/shard_map/all_to_all | solution.py:79
  280.6 10.3 %rev.13 = f32[128,32,128]{0,2,1:T(8,128)} reverse(f32[128,32,128]{0,2,1:T(8,128)S(1)} %get-tuple-element.4), dimensions={1,2} | reverse | bytes 4194304 | tf_op jit(solution)/shard_map/jit(_flip)/rev | solution.py:78
  290.9 37.5 %all-to-all-done.1 = f32[128,16,256]{0,2,1:T(8,128)} async-done(((f32[128,16,256]{0,2,1:T(8,128)}), f32[128,16,256]{0,2,1:T(8,128)}, u32[]{:S(2)}, u32[]{:S(2)}) %all-to-all-start.1) | async-done | bytes 2097184 | tf_op jit(solution)/shard_map/all_to_all | solution.py:79
  328.4 4.8 %all-to-all-start.3 = ((f32[128,16,256]{0,2,1:T(8,128)}), f32[128,16,256]{0,2,1:T(8,128)}, u32[]{:S(2)}, u32[]{:S(2)}) async-start(f32[128,16,256]{0,2,1:T(8,128)} %bitcast.122), calls=%async_computation.3 | async-start | bytes 4194304 | tf_op jit(solution)/shard_map/all_to_all | solution.py:79
  333.3 47.7 %all-to-all-done.3 = f32[128,16,256]{0,2,1:T(8,128)} async-done(((f32[128,16,256]{0,2,1:T(8,128)}), f32[128,16,256]{0,2,1:T(8,128)}, u32[]{:S(2)}, u32[]{:S(2)}) %all-to-all-start.3) | async-done | bytes 2097184 | tf_op jit(solution)/shard_map/all_to_all | solution.py:79
  380.9 5.2 %fusion.64 = (f32[256,2048]{1,0:T(8,128)S(1)}, f32[256,2048]{1,0:T(8,128)S(1)}, f32[256,2048]{1,0:T(8,128)S(1)}, f32[256,2048]{1,0:T(8,128)S(1)}) fusion(f32[256,2048]{1,0:T(8,128)} %get-tuple-element.13, f32[256,2048]{1,0:T(8,128)} %fusion.82, f32[256,2048]{1,0:T(8,128)} %get-tuple-element.18, f32[2048]{0:T(1024)S(1)} %copy-done.31, ...), kind=kLoop, calls=%fused_computation.189 | loop fusion | flops 4194304 | bytes 20979712 | tf_op jit(solution)/shard_map/mul | solution.py:150
  386.6 3.2 collective-permute-start.1
  389.8 11.6 %convolution_convert_fusion = bf16[256,4096]{1,0:T(8,128)(2,1)} fusion(bf16[2048,4096]{1,0:T(8,128)(2,1)} %all-gather.2.cloned.1.call-done, f32[256,2048]{1,0:T(8,128)S(1)} %copy-done.6, f32[256,2048]{1,0:T(8,128)S(1)} %get-tuple-element.20), kind=kOutput, calls=%fused_computation | convolution fusion | flops 4297064448 | bytes 23068672 | tf_op jit(solution)/shard_map/dot_general | solution.py:138
  401.5 1.9 fusion.24
  403.4 4.2 %fusion.14 = (bf16[256,2048]{1,0:T(8,128)(2,1)}, bf16[256,2048]{1,0:T(8,128)(2,1)}) fusion(f32[256,2048]{1,0:T(8,128)S(1)} %mul.732, f32[2,2048]{1,0:T(2,128)S(1)} %get-tuple-element.30, f32[256]{0:T(256)S(1)} %get-tuple-element.71, f32[256]{0:T(256)S(1)} %get-tuple-element.70, f32[2048]{0:T(1024)S(1)} %bitcast.140, f32[2048]{0:T(1024)S(1)} %bitcast.142, ...), kind=kLoop, calls=%fused_computation.19 | loop fusion | flops 10485760 | bytes 6375424 | tf_op jit(solution)/shard_map/convert_element_type | solution.py:162
  (263 shorter events, 17.1 us)
Async XLA Ops:
  7.2 165.0 %copy-start = (bf16[256,4096]{1,0:T(8,128)(2,1)S(1)}, bf16[256,4096]{1,0:T(8,128)(2,1)}, u32[]{:S(2)}) copy-start(bf16[256,4096]{1,0:T(8,128)(2,1)} %param.18) | copy-start | bytes 6291460
  7.2 10.4 %copy-start.7 = (bf16[256,2048]{1,0:T(8,128)(2,1)S(1)}, bf16[256,2048]{1,0:T(8,128)(2,1)}, u32[]{:S(2)}) copy-start(bf16[256,2048]{1,0:T(8,128)(2,1)} %param.11) | copy-start | bytes 3145732
  7.2 165.0 %all-gather.2.cloned.1.call-start = ((), (), s32[]{:S(2)}) async-start(), calls=%async_computation.4 | async-start | bytes 17825792 | tf_op jit(solution)/shard_map/all_gather | solution.py:137
  9.6 7.4 %collective-permute-start = (bf16[3,2,2048]{2,1,0:T(2,128)(2,1)S(1)}, bf16[3,2,2048]{2,1,0:T(2,128)(2,1)S(1)}, u32[]{:S(2)}, u32[]{:S(2)}) collective-permute-start(bf16[3,2,2048]{2,1,0:T(2,128)(2,1)S(1)} %pad_maximum_fusion.3), channel_id=1, source_target_pairs={{0,1},{1,2},{2,3},{3,4},{4,5},{5,6},{6,7},{7,8},{8,9},{9,10},{10,1... | collective-permute-start | bytes 73736 | tf_op jit(solution)/shard_map/ppermute | solution.py:13
  12.9 4.9 %copy-start.8 = (bf16[256,2048]{1,0:T(8,128)(2,1)S(1)}, bf16[256,2048]{1,0:T(8,128)(2,1)}, u32[]{:S(2)}) copy-start(bf16[256,2048]{1,0:T(8,128)(2,1)} %param.12) | copy-start | bytes 3145732
  22.9 15.1 %copy-start.9 = (bf16[256,2048]{1,0:T(8,128)(2,1)S(1)}, bf16[256,2048]{1,0:T(8,128)(2,1)}, u32[]{:S(2)}) copy-start(bf16[256,2048]{1,0:T(8,128)(2,1)} %param.10) | copy-start | bytes 3145732
  22.9 86.3 %all-to-all-start = ((f32[16,128,256]{1,2,0:T(8,128)}), f32[16,128,256]{1,2,0:T(8,128)}, u32[]{:S(2)}, u32[]{:S(2)}) async-start(f32[16,128,256]{1,2,0:T(8,128)} %bitcast.121), calls=%async_computation | async-start | bytes 4194304 | tf_op jit(solution)/shard_map/all_to_all | solution.py:59
  31.6 5.5 %copy-start.36 = (f32[32]{0:T(128)}, f32[32]{0:T(128)S(1)}, u32[]{:S(2)}) copy-start(f32[32]{0:T(128)S(1)} %broadcast_subtract_fusion.1) | copy-start | bytes 388
  31.6 5.5 %copy-start.38 = (f32[32]{0:T(128)}, f32[32]{0:T(128)S(1)}, u32[]{:S(2)}) copy-start(f32[32]{0:T(128)S(1)} %convert_subtract_fusion) | copy-start | bytes 388
  112.1 69.5 %copy-start.18 = (f32[1,1,2048]{2,1,0:T(1,128)S(1)}, f32[1,1,2048]{2,1,0:T(1,128)}, u32[]{:S(2)}) copy-start(f32[1,1,2048]{2,1,0:T(1,128)} %get-tuple-element.25) | copy-start | bytes 24580
  112.1 69.5 %copy-start.19 = (f32[1,1,2048]{2,1,0:T(1,128)S(1)}, f32[1,1,2048]{2,1,0:T(1,128)}, u32[]{:S(2)}) copy-start(f32[1,1,2048]{2,1,0:T(1,128)} %get-tuple-element.26) | copy-start | bytes 24580
  112.1 69.5 %copy-start.20 = (f32[1,1,2048]{2,1,0:T(1,128)S(1)}, f32[1,1,2048]{2,1,0:T(1,128)}, u32[]{:S(2)}) copy-start(f32[1,1,2048]{2,1,0:T(1,128)} %get-tuple-element.27) | copy-start | bytes 24580
  112.1 69.5 %copy-start.28 = (f32[256]{0:T(256)S(1)}, f32[256]{0:T(256)}, u32[]{:S(2)}) copy-start(f32[256]{0:T(256)} %copy-done.27) | copy-start | bytes 3076
  112.1 69.5 %copy-start.30 = (f32[256]{0:T(256)S(1)}, f32[256]{0:T(256)}, u32[]{:S(2)}) copy-start(f32[256]{0:T(256)} %copy-done.29) | copy-start | bytes 3076
  190.0 6.7 %copy-start.2 = (f32[128,32,128]{2,0,1:T(8,128)S(1)}, f32[128,32,128]{2,0,1:T(8,128)}, u32[]{:S(2)}) copy-start(f32[128,32,128]{2,0,1:T(8,128)} %copy.23) | copy-start | bytes 6291460
  190.0 54.5 %all-to-all-start.2 = ((f32[16,128,256]{1,2,0:T(8,128)}), f32[16,128,256]{1,2,0:T(8,128)}, u32[]{:S(2)}, u32[]{:S(2)}) async-start(f32[16,128,256]{1,2,0:T(8,128)} %bitcast.120), calls=%async_computation.2 | async-start | bytes 4194304 | tf_op jit(solution)/shard_map/all_to_all | solution.py:59
  196.7 5.0 %copy-start.23 = (f32[2,128,16]{1,2,0:T(8,128)S(1)}, f32[2,128,16]{1,2,0:T(8,128)}, u32[]{:S(2)}) copy-start(f32[2,128,16]{1,2,0:T(8,128)} %slice.491) | copy-start | bytes 49156
  196.7 5.0 %copy-start.24 = (f32[2,128,16]{1,2,0:T(8,128)S(1)}, f32[2,128,16]{1,2,0:T(8,128)}, u32[]{:S(2)}) copy-start(f32[2,128,16]{1,2,0:T(8,128)} %slice.490) | copy-start | bytes 49156
  196.7 6.0 %copy-start.26 = (f32[2,128,15]{1,2,0:T(8,128)S(1)}, f32[2,128,15]{1,2,0:T(8,128)}, u32[]{:S(2)}) copy-start(f32[2,128,15]{1,2,0:T(8,128)} %slice.510) | copy-start | bytes 46084
  196.7 6.0 %copy-start.35 = (f32[2,128,1]{1,2,0:T(1,128)S(1)}, f32[2,128,1]{1,2,0:T(1,128)}, u32[]{:S(2)}) copy-start(f32[2,128,1]{1,2,0:T(1,128)} %slice.607) | copy-start | bytes 3076
  196.7 6.2 %copy-start.39 = (f32[32]{0:T(128)S(1)}, f32[32]{0:T(128)}, u32[]{:S(2)}) copy-start(f32[32]{0:T(128)} %copy-done.38) | copy-start | bytes 388
  262.9 5.0 %copy-start.21 = (f32[2,128,16]{1,2,0:T(8,128)S(1)}, f32[2,128,16]{1,2,0:T(8,128)}, u32[]{:S(2)}) copy-start(f32[2,128,16]{1,2,0:T(8,128)} %slice.539) | copy-start | bytes 49156
  262.9 5.0 %copy-start.22 = (f32[2,128,16]{1,2,0:T(8,128)S(1)}, f32[2,128,16]{1,2,0:T(8,128)}, u32[]{:S(2)}) copy-start(f32[2,128,16]{1,2,0:T(8,128)} %slice.538) | copy-start | bytes 49156
  262.9 6.0 %copy-start.25 = (f32[2,128,15]{1,2,0:T(8,128)S(1)}, f32[2,128,15]{1,2,0:T(8,128)}, u32[]{:S(2)}) copy-start(f32[2,128,15]{1,2,0:T(8,128)} %slice.558) | copy-start | bytes 46084
  262.9 6.0 %copy-start.34 = (f32[2,128,1]{1,2,0:T(1,128)S(1)}, f32[2,128,1]{1,2,0:T(1,128)}, u32[]{:S(2)}) copy-start(f32[2,128,1]{1,2,0:T(1,128)} %slice.639) | copy-start | bytes 3076
  262.9 6.1 %copy-start.37 = (f32[32]{0:T(128)S(1)}, f32[32]{0:T(128)}, u32[]{:S(2)}) copy-start(f32[32]{0:T(128)} %copy-done.36) | copy-start | bytes 388
  262.9 6.2 %copy-start.33 = (f32[2,128]{1,0:T(2,128)S(1)}, f32[2,128]{1,0:T(2,128)}, u32[]{:S(2)}) copy-start(f32[2,128]{1,0:T(2,128)} %get-tuple-element.15) | copy-start | bytes 3076
  275.9 52.4 %all-to-all-start.1 = ((f32[128,16,256]{0,2,1:T(8,128)}), f32[128,16,256]{0,2,1:T(8,128)}, u32[]{:S(2)}, u32[]{:S(2)}) async-start(f32[128,16,256]{0,2,1:T(8,128)} %bitcast.119), calls=%async_computation.1 | async-start | bytes 4194304 | tf_op jit(solution)/shard_map/all_to_all | solution.py:79
  328.4 52.6 %copy-start.3 = (f32[256,2048]{1,0:T(8,128)S(1)}, f32[256,2048]{1,0:T(8,128)}, u32[]{:S(2)}) copy-start(f32[256,2048]{1,0:T(8,128)} %get-tuple-element.14) | copy-start | bytes 6291460
  328.4 52.6 %copy-start.31 = (f32[2048]{0:T(1024)S(1)}, f32[2048]{0:T(1024)}, u32[]{:S(2)}) copy-start(f32[2048]{0:T(1024)} %param.16) | copy-start | bytes 24580
  328.4 52.6 %all-to-all-start.3 = ((f32[128,16,256]{0,2,1:T(8,128)}), f32[128,16,256]{0,2,1:T(8,128)}, u32[]{:S(2)}, u32[]{:S(2)}) async-start(f32[128,16,256]{0,2,1:T(8,128)} %bitcast.122), calls=%async_computation.3 | async-start | bytes 4194304 | tf_op jit(solution)/shard_map/all_to_all | solution.py:79
  386.6 14.8 %collective-permute-start.1 = (bf16[3,2,2048]{2,1,0:T(2,128)(2,1)S(1)}, bf16[3,2,2048]{2,1,0:T(2,128)(2,1)S(1)}, u32[]{:S(2)}, u32[]{:S(2)}) collective-permute-start(bf16[3,2,2048]{2,1,0:T(2,128)(2,1)S(1)} %pad_maximum_fusion.4), channel_id=1, source_target_pairs={{1,0},{2,1},{3,2},{4,3},{5,4},{6,5},{7,6},{8,7},{9,8},{10,9},{11,1... | collective-permute-start | bytes 73736 | tf_op jit(solution)/shard_map/ppermute | solution.py:13
  (15 other events, 32.8 us)
Sparse Core Ops, SparseCore 0:
  10.2 161.9 all-gather.1
where the time goes:
time: 416 us; the launch traced here: 414 us
  waiting for transfers between devices  256 us (62%)
  local copies, waits for them, and re-layouts  49.7 us (12%)
  other arithmetic  38.9 us (9%)
  starting transfers between devices  28 us (7%)
  matrix products  26.6 us (6%)
  between operations  15.2 us (4%)
    all_to_all x2, waiting for transfers between devices, relay_pass(): lax.all_to_all(columns, 'seq', split_axis=0, concat_axis=1, tiled=True)  110 us
    all_to_all x2, waiting for transfers between devices, relay_pass(): lax.all_to_all(result.reshape(share_width, block_count * BLOCK), 'seq', s...  85.2 us
    all_gather x1, waiting for transfers between devices, on_device(): weight_piece = lax.all_gather(out_weight, 'seq', axis=0, tiled=True)  60 us
    rev x2, local copies, waits for them, and re-layouts, relay_pass(): blocked = jnp.flip(blocked, axis=(1, 2))  18.5 us
    all_to_all x2, starting transfers between devices, relay_pass(): lax.all_to_all(columns, 'seq', split_axis=0, concat_axis=1, tiled=True)  13.3 us
    dot_general x1, matrix products, on_device(): jnp.dot(gated_rows, weight_piece, preferred_element_type=jnp.float32)  11.6 us
    rev x1, local copies, waits for them, and re-layouts, relay_pass(): result = jnp.flip(result, axis=(1, 2))  10.3 us
    unnamed x2, other arithmetic  9.89 us
  transfers between devices with their start and end apart: 7, of which 5 were waited for; matrix products, arithmetic and copies ran while one was open for 13% of the time, Pallas kernels for 0%

commit v1 on v0

--- a/solution.py
+++ b/solution.py
@@ -134,7 +134,12 @@
         long_conv(product.T, decay_rates, filter_weight, doc_blocks, False).T + skip_gain * product
     )
     gated_rows = (q_short * conv_out).astype(jnp.bfloat16)
-    weight_piece = lax.all_gather(out_weight, "seq", axis=0, tiled=True)
+    ring = [out_weight]
+    for hop in range(15):
+        ring.append(lax.ppermute(ring[-1], "seq", [(dev, (dev + 1) % 16) for dev in range(16)]))
+    weight_piece = jnp.roll(
+        jnp.concatenate(ring[::-1], axis=0), (lax.axis_index("seq") + 1) * ring[0].shape[0], axis=0
+    )
     total_out = jnp.dot(gated_rows, weight_piece, preferred_element_type=jnp.float32)
     column = lax.dot_general(
         cotangent, weight_piece, (((1,), (1,)), ((), ())), preferred_element_type=jnp.float32

time: 416 us -> 578 us (1.39)
  waiting for transfers between devices: 256 us -> 357 us
  local copies, waits for them, and re-layouts: 49.7 us -> 107 us
  starting transfers between devices: 28 us -> 45 us
  between operations: 15.2 us -> 1.91 us
    ppermute x0 -> x15, waiting for transfers between devices: none -> 231 us  [on_device(): lax.ppermute(ring[-1], 'seq', [(dev, (dev + 1) % 16) for dev in range(16)])]
    all_to_all x2, waiting for transfers between devices: 110 us -> 41.2 us  [relay_pass(): lax.all_to_all(columns, 'seq', split_axis=0, concat_axis=1, tiled=True)]
    all_gather x1 -> x0, waiting for transfers between devices: 60 us -> none  [on_device(): weight_piece = lax.all_gather(out_weight, 'seq', axis=0, tiled=True)]
    unnamed x84 -> x145, local copies, waits for them, and re-layouts: 4.31 us -> 60.8 us
    all_to_all x2, starting transfers between devices: 13.3 us -> 30 us  [relay_pass(): lax.all_to_all(columns, 'seq', split_axis=0, concat_axis=1, tiled=True)]
  transfers between devices with their start and end apart: 7 -> 21, of which waited for: 5 -> 17; matrix products, arithmetic and copies ran while one was open for 13% -> 10% of each run, Pallas kernels for 0% -> 0%
where the time goes in v1:
time: 578 us; the launch traced here: 575 us
  waiting for transfers between devices  357 us (62%)
  local copies, waits for them, and re-layouts  107 us (19%)
  starting transfers between devices  45 us (8%)
  other arithmetic  37.5 us (6%)
  matrix products  26.2 us (5%)
    ppermute x15, waiting for transfers between devices, on_device(): lax.ppermute(ring[-1], 'seq', [(dev, (dev + 1) % 16) for dev in range(16)])  231 us
    all_to_all x2, waiting for transfers between devices, relay_pass(): lax.all_to_all(result.reshape(share_width, block_count * BLOCK), 'seq', s...  85.2 us
    unnamed x145, local copies, waits for them, and re-layouts  60.8 us
    all_to_all x2, waiting for transfers between devices, relay_pass(): lax.all_to_all(columns, 'seq', split_axis=0, concat_axis=1, tiled=True)  41.2 us
    all_to_all x2, starting transfers between devices, relay_pass(): lax.all_to_all(columns, 'seq', split_axis=0, concat_axis=1, tiled=True)  30 us
    rev x2, local copies, waits for them, and re-layouts, relay_pass(): blocked = jnp.flip(blocked, axis=(1, 2))  18.4 us
    dot_general x1, matrix products, on_device(): jnp.dot(gated_rows, weight_piece, preferred_element_type=jnp.float32)  12.3 us
  transfers between devices with their start and end apart: 21, of which 17 were waited for; matrix products, arithmetic and copies ran while one was open for 10% of the time, Pallas kernels for 0%

profile of v1, /device:TPU:16, one launch (start us, length us, event | category | flops | bytes accessed | tf_op | source)
XLA Modules:
  0.0 575.4 jit_solution(17986462289365130516)
XLA Ops:
  0.7 15.3 %collective-permute-done.1 = bf16[128,4096]{1,0:T(8,128)(2,1)S(1)} collective-permute-done((bf16[128,4096]{1,0:T(8,128)(2,1)}, bf16[128,4096]{1,0:T(8,128)(2,1)S(1)}, u32[]{:S(2)}, u32[]{:S(2)}) %collective-permute-start.1) | collective-permute-done | bytes 1048608 | tf_op jit(solution)/shard_map/ppermute | solution.py:139
  16.0 15.1 %collective-permute-done.2 = bf16[128,4096]{1,0:T(8,128)(2,1)S(1)} collective-permute-done((bf16[128,4096]{1,0:T(8,128)(2,1)S(1)}, bf16[128,4096]{1,0:T(8,128)(2,1)S(1)}, u32[]{:S(2)}, u32[]{:S(2)}) %collective-permute-start.2) | collective-permute-done | bytes 1048608 | tf_op jit(solution)/shard_map/ppermute | solution.py:139
  32.2 15.1 %collective-permute-done.3 = bf16[128,4096]{1,0:T(8,128)(2,1)S(1)} collective-permute-done((bf16[128,4096]{1,0:T(8,128)(2,1)S(1)}, bf16[128,4096]{1,0:T(8,128)(2,1)S(1)}, u32[]{:S(2)}, u32[]{:S(2)}) %collective-permute-start.3) | collective-permute-done | bytes 1048608 | tf_op jit(solution)/shard_map/ppermute | solution.py:139
  48.3 15.1 %collective-permute-done.4 = bf16[128,4096]{1,0:T(8,128)(2,1)S(1)} collective-permute-done((bf16[128,4096]{1,0:T(8,128)(2,1)S(1)}, bf16[128,4096]{1,0:T(8,128)(2,1)S(1)}, u32[]{:S(2)}, u32[]{:S(2)}) %collective-permute-start.4) | collective-permute-done | bytes 1048608 | tf_op jit(solution)/shard_map/ppermute | solution.py:139
  64.4 15.1 %collective-permute-done.5 = bf16[128,4096]{1,0:T(8,128)(2,1)S(1)} collective-permute-done((bf16[128,4096]{1,0:T(8,128)(2,1)S(1)}, bf16[128,4096]{1,0:T(8,128)(2,1)S(1)}, u32[]{:S(2)}, u32[]{:S(2)}) %collective-permute-start.5) | collective-permute-done | bytes 1048608 | tf_op jit(solution)/shard_map/ppermute | solution.py:139
  80.5 15.1 %collective-permute-done.6 = bf16[128,4096]{1,0:T(8,128)(2,1)S(1)} collective-permute-done((bf16[128,4096]{1,0:T(8,128)(2,1)S(1)}, bf16[128,4096]{1,0:T(8,128)(2,1)S(1)}, u32[]{:S(2)}, u32[]{:S(2)}) %collective-permute-start.6) | collective-permute-done | bytes 1048608 | tf_op jit(solution)/shard_map/ppermute | solution.py:139
  96.6 15.1 %collective-permute-done.7 = bf16[128,4096]{1,0:T(8,128)(2,1)S(1)} collective-permute-done((bf16[128,4096]{1,0:T(8,128)(2,1)S(1)}, bf16[128,4096]{1,0:T(8,128)(2,1)S(1)}, u32[]{:S(2)}, u32[]{:S(2)}) %collective-permute-start.7) | collective-permute-done | bytes 1048608 | tf_op jit(solution)/shard_map/ppermute | solution.py:139
  113.5 14.4 %collective-permute-done.8 = bf16[128,4096]{1,0:T(8,128)(2,1)} collective-permute-done((bf16[128,4096]{1,0:T(8,128)(2,1)S(1)}, bf16[128,4096]{1,0:T(8,128)(2,1)}, u32[]{:S(2)}, u32[]{:S(2)}) %collective-permute-start.8) | collective-permute-done | bytes 1048608 | tf_op jit(solution)/shard_map/ppermute | solution.py:139
  133.6 9.7 %collective-permute-done.9 = bf16[128,4096]{1,0:T(8,128)(2,1)} collective-permute-done((bf16[128,4096]{1,0:T(8,128)(2,1)}, bf16[128,4096]{1,0:T(8,128)(2,1)}, u32[]{:S(2)}, u32[]{:S(2)}) %collective-permute-start.9) | collective-permute-done | bytes 1048608 | tf_op jit(solution)/shard_map/ppermute | solution.py:139
  145.8 12.8 %collective-permute-done.10 = bf16[128,4096]{1,0:T(8,128)(2,1)S(1)} collective-permute-done((bf16[128,4096]{1,0:T(8,128)(2,1)}, bf16[128,4096]{1,0:T(8,128)(2,1)S(1)}, u32[]{:S(2)}, u32[]{:S(2)}) %collective-permute-start.10) | collective-permute-done | bytes 1048608 | tf_op jit(solution)/shard_map/ppermute | solution.py:139
  161.4 12.5 %collective-permute-done.11 = bf16[128,4096]{1,0:T(8,128)(2,1)} collective-permute-done((bf16[128,4096]{1,0:T(8,128)(2,1)S(1)}, bf16[128,4096]{1,0:T(8,128)(2,1)}, u32[]{:S(2)}, u32[]{:S(2)}) %collective-permute-start.11) | collective-permute-done | bytes 1048608 | tf_op jit(solution)/shard_map/ppermute | solution.py:139
  173.9 3.2 multiply_bitcast_fusion.1
  178.7 25.4 %all-to-all-start = ((f32[16,128,256]{1,2,0:T(8,128)}), f32[16,128,256]{1,2,0:T(8,128)}, u32[]{:S(2)}, u32[]{:S(2)}) async-start(f32[16,128,256]{1,2,0:T(8,128)} %bitcast.121), calls=%async_computation | async-start | bytes 4194304 | tf_op jit(solution)/shard_map/all_to_all | solution.py:59
  204.2 58.9 %collective-permute-done.13 = bf16[128,4096]{1,0:T(8,128)(2,1)} collective-permute-done((bf16[128,4096]{1,0:T(8,128)(2,1)}, bf16[128,4096]{1,0:T(8,128)(2,1)}, u32[]{:S(2)}, u32[]{:S(2)}) %collective-permute-start.13) | collective-permute-done | bytes 1048608 | tf_op jit(solution)/shard_map/ppermute | solution.py:139
  265.9 12.7 %collective-permute-done.14 = bf16[128,4096]{1,0:T(8,128)(2,1)} collective-permute-done((bf16[128,4096]{1,0:T(8,128)(2,1)}, bf16[128,4096]{1,0:T(8,128)(2,1)}, u32[]{:S(2)}, u32[]{:S(2)}) %collective-permute-start.14) | collective-permute-done | bytes 1048608 | tf_op jit(solution)/shard_map/ppermute | solution.py:139
  284.3 2.9 maximum_convert_fusion
  287.1 2.9 copy.23
  290.1 3.9 collective-permute-done.15
  345.9 8.3 %fusion.11 = f32[256,2048]{1,0:T(8,128)S(1)} fusion(bf16[256,4096]{1,0:T(8,128)(2,1)S(1)} %copy-done, bf16[4096,4096]{1,0:T(8,128)(2,1)} %constant_dynamic-update-slice_fusion, s32[]{:T(128)S(6)} %select_n.21), kind=kOutput, calls=%fused_computation.11 | convolution fusion | flops 4294967296 | bytes 20971524 | tf_op jit(solution)/shard_map/dot_general | solution.py:144
  358.0 4.7 all-to-all-start.2
  368.9 41.2 %all-to-all-done.2 = f32[16,128,256]{1,2,0:T(8,128)} async-done(((f32[16,128,256]{1,2,0:T(8,128)}), f32[16,128,256]{1,2,0:T(8,128)}, u32[]{:S(2)}, u32[]{:S(2)}) %all-to-all-start.2) | async-done | bytes 2097184 | tf_op jit(solution)/shard_map/all_to_all | solution.py:59
  410.1 16.5 %rev.11 = f32[128,32,128]{0,2,1:T(8,128)} reverse(f32[128,32,128]{0,2,1:T(8,128)} %bitcast.33), dimensions={1,2} | reverse | bytes 4194304 | tf_op jit(solution)/shard_map/jit(_flip)/rev | solution.py:70
  434.7 6.9 %multiply_reduce_fusion = (f32[128,32,128]{0,2,1:T(8,128)S(1)}, f32[128,32,128]{0,2,1:T(8,128)}) fusion(f32[2,128,32,128]{1,3,2,0:T(8,128)} %copy-done.6, f32[2,128,32]{1,2,0:T(8,128)S(1)} %pad_multiply_fusion, f32[2,128]{1,0:T(2,128)S(1)} %copy-done.48, f32[2,128,128]{1,2,0:T(8,128)S(1)} %get-tuple-element.90, f32[2,128,32,128]{1,3,2,0:T(8,128)} %copy-done.5, ...), kind=kLoop, calls=%fused_computation.5 | loop fusion | flops 7340032 | bytes 12780544 | tf_op jit(solution)/shard_map/reduce_sum | solution.py:54
  441.6 4.7 all-to-all-start.1
  446.2 10.2 %rev.13 = f32[128,32,128]{0,2,1:T(8,128)} reverse(f32[128,32,128]{0,2,1:T(8,128)S(1)} %get-tuple-element.4), dimensions={1,2} | reverse | bytes 4194304 | tf_op jit(solution)/shard_map/jit(_flip)/rev | solution.py:78
  456.4 37.5 %all-to-all-done.1 = f32[128,16,256]{0,2,1:T(8,128)} async-done(((f32[128,16,256]{0,2,1:T(8,128)}), f32[128,16,256]{0,2,1:T(8,128)}, u32[]{:S(2)}, u32[]{:S(2)}) %all-to-all-start.1) | async-done | bytes 2097184 | tf_op jit(solution)/shard_map/all_to_all | solution.py:79
  494.0 4.8 all-to-all-start.3
  498.9 47.7 %all-to-all-done.3 = f32[128,16,256]{0,2,1:T(8,128)} async-done(((f32[128,16,256]{0,2,1:T(8,128)}), f32[128,16,256]{0,2,1:T(8,128)}, u32[]{:S(2)}, u32[]{:S(2)}) %all-to-all-start.3) | async-done | bytes 2097184 | tf_op jit(solution)/shard_map/all_to_all | solution.py:79
  546.6 6.7 %fusion.76 = (f32[256,2048]{1,0:T(8,128)S(1)}, f32[256,2048]{1,0:T(8,128)S(1)}, f32[256,2048]{1,0:T(8,128)S(1)}, f32[256,2048]{1,0:T(8,128)}) fusion(f32[256,2048]{1,0:T(8,128)} %get-tuple-element.13, f32[256,2048]{1,0:T(8,128)} %copy-done.8, f32[256,2048]{1,0:T(8,128)} %get-tuple-element.18, f32[2048]{0:T(1024)S(1)} %copy-done.46, ...), kind=kLoop, calls=%fused_computation.228 | loop fusion | flops 4194304 | bytes 20979712 | tf_op jit(solution)/shard_map/mul | solution.py:155
  553.6 3.2 collective-permute-start.16
  556.8 12.3 %fusion.4 = bf16[256,4096]{1,0:T(8,128)(2,1)} fusion(bf16[4096,4096]{1,0:T(8,128)(2,1)} %constant_dynamic-update-slice_fusion, s32[]{:T(128)S(6)} %select_n.21, f32[256,2048]{1,0:T(8,128)S(1)} %copy-done.7, f32[256,2048]{1,0:T(8,128)} %get-tuple-element.20), kind=kOutput, calls=%fused_computation.4 | convolution fusion | flops 4297064448 | bytes 23068676 | tf_op jit(solution)/shard_map/dot_general | solution.py:143
  571.2 4.2 fusion.24
  (352 shorter events, 99.3 us)
Async XLA Ops:
  0.6 345.2 %copy-start = (bf16[256,4096]{1,0:T(8,128)(2,1)S(1)}, bf16[256,4096]{1,0:T(8,128)(2,1)}, u32[]{:S(2)}) copy-start(bf16[256,4096]{1,0:T(8,128)(2,1)} %param.18) | copy-start | bytes 6291460
  0.6 15.4 %collective-permute-start.1 = (bf16[128,4096]{1,0:T(8,128)(2,1)}, bf16[128,4096]{1,0:T(8,128)(2,1)S(1)}, u32[]{:S(2)}, u32[]{:S(2)}) collective-permute-start(bf16[128,4096]{1,0:T(8,128)(2,1)} %param.17), channel_id=1, source_target_pairs={{0,1},{1,2},{2,3},{3,4},{4,5},{5,6},{6,7},{7,8},{8,9},{9,10},{10,1... | collective-permute-start | bytes 3145736 | tf_op jit(solution)/shard_map/ppermute | solution.py:139
  16.0 15.1 %collective-permute-start.2 = (bf16[128,4096]{1,0:T(8,128)(2,1)S(1)}, bf16[128,4096]{1,0:T(8,128)(2,1)S(1)}, u32[]{:S(2)}, u32[]{:S(2)}) collective-permute-start(bf16[128,4096]{1,0:T(8,128)(2,1)S(1)} %collective-permute-done.1), channel_id=1, source_target_pairs={{0,1},{1,2},{2,3},{3,4},{4,5},{5,6},{6,7},{7,8},{8,9},{9,10},{10,1... | collective-permute-start | bytes 3145736 | tf_op jit(solution)/shard_map/ppermute | solution.py:139
  32.2 15.1 %collective-permute-start.3 = (bf16[128,4096]{1,0:T(8,128)(2,1)S(1)}, bf16[128,4096]{1,0:T(8,128)(2,1)S(1)}, u32[]{:S(2)}, u32[]{:S(2)}) collective-permute-start(bf16[128,4096]{1,0:T(8,128)(2,1)S(1)} %collective-permute-done.2), channel_id=1, source_target_pairs={{0,1},{1,2},{2,3},{3,4},{4,5},{5,6},{6,7},{7,8},{8,9},{9,10},{10,1... | collective-permute-start | bytes 3145736 | tf_op jit(solution)/shard_map/ppermute | solution.py:139
  48.3 15.1 %collective-permute-start.4 = (bf16[128,4096]{1,0:T(8,128)(2,1)S(1)}, bf16[128,4096]{1,0:T(8,128)(2,1)S(1)}, u32[]{:S(2)}, u32[]{:S(2)}) collective-permute-start(bf16[128,4096]{1,0:T(8,128)(2,1)S(1)} %collective-permute-done.3), channel_id=1, source_target_pairs={{0,1},{1,2},{2,3},{3,4},{4,5},{5,6},{6,7},{7,8},{8,9},{9,10},{10,1... | collective-permute-start | bytes 3145736 | tf_op jit(solution)/shard_map/ppermute | solution.py:139
  64.4 15.1 %collective-permute-start.5 = (bf16[128,4096]{1,0:T(8,128)(2,1)S(1)}, bf16[128,4096]{1,0:T(8,128)(2,1)S(1)}, u32[]{:S(2)}, u32[]{:S(2)}) collective-permute-start(bf16[128,4096]{1,0:T(8,128)(2,1)S(1)} %collective-permute-done.4), channel_id=1, source_target_pairs={{0,1},{1,2},{2,3},{3,4},{4,5},{5,6},{6,7},{7,8},{8,9},{9,10},{10,1... | collective-permute-start | bytes 3145736 | tf_op jit(solution)/shard_map/ppermute | solution.py:139
  80.5 15.1 %collective-permute-start.6 = (bf16[128,4096]{1,0:T(8,128)(2,1)S(1)}, bf16[128,4096]{1,0:T(8,128)(2,1)S(1)}, u32[]{:S(2)}, u32[]{:S(2)}) collective-permute-start(bf16[128,4096]{1,0:T(8,128)(2,1)S(1)} %collective-permute-done.5), channel_id=1, source_target_pairs={{0,1},{1,2},{2,3},{3,4},{4,5},{5,6},{6,7},{7,8},{8,9},{9,10},{10,1... | collective-permute-start | bytes 3145736 | tf_op jit(solution)/shard_map/ppermute | solution.py:139
  96.6 15.1 %collective-permute-start.7 = (bf16[128,4096]{1,0:T(8,128)(2,1)S(1)}, bf16[128,4096]{1,0:T(8,128)(2,1)S(1)}, u32[]{:S(2)}, u32[]{:S(2)}) collective-permute-start(bf16[128,4096]{1,0:T(8,128)(2,1)S(1)} %collective-permute-done.6), channel_id=1, source_target_pairs={{0,1},{1,2},{2,3},{3,4},{4,5},{5,6},{6,7},{7,8},{8,9},{9,10},{10,1... | collective-permute-start | bytes 3145736 | tf_op jit(solution)/shard_map/ppermute | solution.py:139
  112.7 15.2 %collective-permute-start.8 = (bf16[128,4096]{1,0:T(8,128)(2,1)S(1)}, bf16[128,4096]{1,0:T(8,128)(2,1)}, u32[]{:S(2)}, u32[]{:S(2)}) collective-permute-start(bf16[128,4096]{1,0:T(8,128)(2,1)S(1)} %collective-permute-done.7), channel_id=1, source_target_pairs={{0,1},{1,2},{2,3},{3,4},{4,5},{5,6},{6,7},{7,8},{8,9},{9,10},{10,1... | collective-permute-start | bytes 3145736 | tf_op jit(solution)/shard_map/ppermute | solution.py:139
  127.9 15.4 %collective-permute-start.9 = (bf16[128,4096]{1,0:T(8,128)(2,1)}, bf16[128,4096]{1,0:T(8,128)(2,1)}, u32[]{:S(2)}, u32[]{:S(2)}) collective-permute-start(bf16[128,4096]{1,0:T(8,128)(2,1)} %collective-permute-done.8), channel_id=1, source_target_pairs={{0,1},{1,2},{2,3},{3,4},{4,5},{5,6},{6,7},{7,8},{8,9},{9,10},{10,1... | collective-permute-start | bytes 3145736 | tf_op jit(solution)/shard_map/ppermute | solution.py:139
  128.7 30.0 %collective-permute-start = (bf16[3,2,2048]{2,1,0:T(2,128)(2,1)S(1)}, bf16[3,2,2048]{2,1,0:T(2,128)(2,1)S(1)}, u32[]{:S(2)}, u32[]{:S(2)}) collective-permute-start(bf16[3,2,2048]{2,1,0:T(2,128)(2,1)S(1)} %pad_maximum_fusion.3), channel_id=1, source_target_pairs={{0,1},{1,2},{2,3},{3,4},{4,5},{5,6},{6,7},{7,8},{8,9},{9,10},{10,1... | collective-permute-start | bytes 73736 | tf_op jit(solution)/shard_map/ppermute | solution.py:13
  132.1 28.9 %copy-start.24 = (bf16[256,2048]{1,0:T(8,128)(2,1)S(1)}, bf16[256,2048]{1,0:T(8,128)(2,1)}, u32[]{:S(2)}) copy-start(bf16[256,2048]{1,0:T(8,128)(2,1)} %param.11) | copy-start | bytes 3145732
  143.3 15.3 %collective-permute-start.10 = (bf16[128,4096]{1,0:T(8,128)(2,1)}, bf16[128,4096]{1,0:T(8,128)(2,1)S(1)}, u32[]{:S(2)}, u32[]{:S(2)}) collective-permute-start(bf16[128,4096]{1,0:T(8,128)(2,1)} %collective-permute-done.9), channel_id=1, source_target_pairs={{0,1},{1,2},{2,3},{3,4},{4,5},{5,6},{6,7},{7,8},{8,9},{9,10},{10,1... | collective-permute-start | bytes 3145736 | tf_op jit(solution)/shard_map/ppermute | solution.py:139
  145.8 28.1 %copy-start.25 = (f32[1,1,2048]{2,1,0:T(1,128)}, f32[1,1,2048]{2,1,0:T(1,128)S(1)}, u32[]{:S(2)}) copy-start(f32[1,1,2048]{2,1,0:T(1,128)S(1)} %get-tuple-element.23) | copy-start | bytes 24580
  145.8 28.1 %copy-start.27 = (f32[1,1,2048]{2,1,0:T(1,128)}, f32[1,1,2048]{2,1,0:T(1,128)S(1)}, u32[]{:S(2)}) copy-start(f32[1,1,2048]{2,1,0:T(1,128)S(1)} %get-tuple-element.24) | copy-start | bytes 24580
  145.8 28.1 %copy-start.29 = (f32[1,1,2048]{2,1,0:T(1,128)}, f32[1,1,2048]{2,1,0:T(1,128)S(1)}, u32[]{:S(2)}) copy-start(f32[1,1,2048]{2,1,0:T(1,128)S(1)} %get-tuple-element.28) | copy-start | bytes 24580
  145.8 28.1 %copy-start.31 = (f32[1,1,2048]{2,1,0:T(1,128)}, f32[1,1,2048]{2,1,0:T(1,128)S(1)}, u32[]{:S(2)}) copy-start(f32[1,1,2048]{2,1,0:T(1,128)S(1)} %get-tuple-element.29) | copy-start | bytes 24580
  158.7 15.2 %collective-permute-start.11 = (bf16[128,4096]{1,0:T(8,128)(2,1)S(1)}, bf16[128,4096]{1,0:T(8,128)(2,1)}, u32[]{:S(2)}, u32[]{:S(2)}) collective-permute-start(bf16[128,4096]{1,0:T(8,128)(2,1)S(1)} %collective-permute-done.10), channel_id=1, source_target_pairs={{0,1},{1,2},{2,3},{3,4},{4,5},{5,6},{6,7},{7,8},{8,9},{9,10},{10,1... | collective-permute-start | bytes 3145736 | tf_op jit(solution)/shard_map/ppermute | solution.py:139
  158.7 15.2 %copy-start.44 = (f32[256]{0:T(256)}, f32[256]{0:T(256)S(1)}, u32[]{:S(2)}) copy-start(f32[256]{0:T(256)S(1)} %get-tuple-element.85) | copy-start | bytes 3076
  173.9 30.1 %collective-permute-start.12 = (bf16[128,4096]{1,0:T(8,128)(2,1)}, bf16[128,4096]{1,0:T(8,128)(2,1)}, u32[]{:S(2)}, u32[]{:S(2)}) collective-permute-start(bf16[128,4096]{1,0:T(8,128)(2,1)} %collective-permute-done.11), channel_id=1, source_target_pairs={{0,1},{1,2},{2,3},{3,4},{4,5},{5,6},{6,7},{7,8},{8,9},{9,10},{10,1... | collective-permute-start | bytes 3145736 | tf_op jit(solution)/shard_map/ppermute | solution.py:139
  178.7 108.5 %all-to-all-start = ((f32[16,128,256]{1,2,0:T(8,128)}), f32[16,128,256]{1,2,0:T(8,128)}, u32[]{:S(2)}, u32[]{:S(2)}) async-start(f32[16,128,256]{1,2,0:T(8,128)} %bitcast.121), calls=%async_computation | async-start | bytes 4194304 | tf_op jit(solution)/shard_map/all_to_all | solution.py:59
  204.0 59.1 %collective-permute-start.13 = (bf16[128,4096]{1,0:T(8,128)(2,1)}, bf16[128,4096]{1,0:T(8,128)(2,1)}, u32[]{:S(2)}, u32[]{:S(2)}) collective-permute-start(bf16[128,4096]{1,0:T(8,128)(2,1)} %collective-permute-done.12), channel_id=1, source_target_pairs={{0,1},{1,2},{2,3},{3,4},{4,5},{5,6},{6,7},{7,8},{8,9},{9,10},{10,1... | collective-permute-start | bytes 3145736 | tf_op jit(solution)/shard_map/ppermute | solution.py:139
  263.1 15.4 %collective-permute-start.14 = (bf16[128,4096]{1,0:T(8,128)(2,1)}, bf16[128,4096]{1,0:T(8,128)(2,1)}, u32[]{:S(2)}, u32[]{:S(2)}) collective-permute-start(bf16[128,4096]{1,0:T(8,128)(2,1)} %collective-permute-done.13), channel_id=1, source_target_pairs={{0,1},{1,2},{2,3},{3,4},{4,5},{5,6},{6,7},{7,8},{8,9},{9,10},{10,1... | collective-permute-start | bytes 3145736 | tf_op jit(solution)/shard_map/ppermute | solution.py:139
  265.3 18.1 %copy-start.53 = (f32[32]{0:T(128)}, f32[32]{0:T(128)S(1)}, u32[]{:S(2)}) copy-start(f32[32]{0:T(128)S(1)} %convert_subtract_fusion) | copy-start | bytes 388
  265.3 18.1 %copy-start.51 = (f32[32]{0:T(128)}, f32[32]{0:T(128)S(1)}, u32[]{:S(2)}) copy-start(f32[32]{0:T(128)S(1)} %broadcast_subtract_fusion.1) | copy-start | bytes 388
  278.5 15.4 %collective-permute-start.15 = (bf16[128,4096]{1,0:T(8,128)(2,1)}, bf16[128,4096]{1,0:T(8,128)(2,1)}, u32[]{:S(2)}, u32[]{:S(2)}) collective-permute-start(bf16[128,4096]{1,0:T(8,128)(2,1)} %collective-permute-done.14), channel_id=1, source_target_pairs={{0,1},{1,2},{2,3},{3,4},{4,5},{5,6},{6,7},{7,8},{8,9},{9,10},{10,1... | collective-permute-start | bytes 3145736 | tf_op jit(solution)/shard_map/ppermute | solution.py:139
  358.0 52.1 %all-to-all-start.2 = ((f32[16,128,256]{1,2,0:T(8,128)}), f32[16,128,256]{1,2,0:T(8,128)}, u32[]{:S(2)}, u32[]{:S(2)}) async-start(f32[16,128,256]{1,2,0:T(8,128)} %bitcast.120), calls=%async_computation.2 | async-start | bytes 4194304 | tf_op jit(solution)/shard_map/all_to_all | solution.py:59
  441.6 52.4 %all-to-all-start.1 = ((f32[128,16,256]{0,2,1:T(8,128)}), f32[128,16,256]{0,2,1:T(8,128)}, u32[]{:S(2)}, u32[]{:S(2)}) async-start(f32[128,16,256]{0,2,1:T(8,128)} %bitcast.119), calls=%async_computation.1 | async-start | bytes 4194304 | tf_op jit(solution)/shard_map/all_to_all | solution.py:79
  494.0 52.6 %copy-start.4 = (f32[256,2048]{1,0:T(8,128)S(1)}, f32[256,2048]{1,0:T(8,128)}, u32[]{:S(2)}) copy-start(f32[256,2048]{1,0:T(8,128)} %get-tuple-element.14) | copy-start | bytes 6291460
  494.0 52.6 %copy-start.46 = (f32[2048]{0:T(1024)S(1)}, f32[2048]{0:T(1024)}, u32[]{:S(2)}) copy-start(f32[2048]{0:T(1024)} %param.16) | copy-start | bytes 24580
  494.0 52.6 %all-to-all-start.3 = ((f32[128,16,256]{0,2,1:T(8,128)}), f32[128,16,256]{0,2,1:T(8,128)}, u32[]{:S(2)}, u32[]{:S(2)}) async-start(f32[128,16,256]{0,2,1:T(8,128)} %bitcast.122), calls=%async_computation.3 | async-start | bytes 4194304 | tf_op jit(solution)/shard_map/all_to_all | solution.py:79
  553.6 15.6 %collective-permute-start.16 = (bf16[3,2,2048]{2,1,0:T(2,128)(2,1)S(1)}, bf16[3,2,2048]{2,1,0:T(2,128)(2,1)S(1)}, u32[]{:S(2)}, u32[]{:S(2)}) collective-permute-start(bf16[3,2,2048]{2,1,0:T(2,128)(2,1)S(1)} %pad_maximum_fusion.4), channel_id=1, source_target_pairs={{1,0},{2,1},{3,2},{4,3},{5,4},{6,5},{7,6},{8,7},{9,8},{10,9},{11,1... | collective-permute-start | bytes 73736 | tf_op jit(solution)/shard_map/ppermute | solution.py:13
  (44 other events, 191.0 us)
